TPU v7x, 32 devices: a whole 2x2x4 slice. The times are simulated.
32 devices in a mesh: dp: 4 (over y, x), mp: 8 (over z, core).
Axes of the slice: x: 2, y: 2, z: 4, core: 2. Of those that a mesh axis runs over, the one named last changes fastest.
Arguments:
- residual: bfloat16 [1024, 4096], P(('dp', 'mp')), may hold values from -6 to 6
- ffn_gain: float32 [4096], replicated, may hold values from 0.5 to 1.5
- gate_weight: bfloat16 [4096, 8192], P(None, 'mp'), may hold values from -0.09375 to 0.09375
- up_weight: bfloat16 [4096, 8192], P(None, 'mp'), may hold values from -0.09375 to 0.09375
- down_weight: bfloat16 [8192, 4096], P('mp'), may hold values from -0.0625 to 0.0625
- final_gain: float32 [4096], replicated, may hold values from 0.5 to 1.5
- head_weight: bfloat16 [4096, 65536], P(None, 'mp')
- passage_ids: int32 [4, 256], P('dp'), may hold values from 0 to 3, never falling along the last dimension, each value on 1 to 128 neighbouring positions
- valid_counts: int32 [4, 4], P('dp'), may hold values from 1 to 128
Outputs:
- term_weights: float32 [16, 65536], P('dp', 'mp')
- entropy: float32 [], replicated
- grad_hidden: float32 [1024, 4096], P(('dp', 'mp'))
Inputs may be any that keep to these rules, and one draw needn't show every extreme that they name: `passage_ids`: within each group the ids never fall and every passage of 0 to 3 has 1 to 128 rows.
All inputs are finite; a program needn't handle non-finite values.
Results may differ from a plain program's by a relative error of at most 0.0069.
The roundings to bfloat16 on the way count: a program that leaves them out, or rounds other values in their place, can miss the bound.
Values may be sent and summed in bfloat16 or wider, within the bound.
A program may use at most 192 MiB of HBM per device.

v0:
```python
import jax
import jax.numpy as jnp
from jax import lax
from jax.sharding import PartitionSpec as P


def rms_scale(values):
    return lax.rsqrt(jnp.mean(values * values, axis=-1, keepdims=True) + 1e-05)


def pool_masks(ids, counts):
    slots = jnp.arange(counts.shape[0], dtype=jnp.int32)
    member = ids[:, None] == slots[None, :]
    starts = jnp.sum((ids[:, None] < slots[None, :]).astype(jnp.int32), axis=0)
    start_row = jnp.sum(jnp.where(member, starts[None, :], 0), axis=1)
    count_row = jnp.sum(jnp.where(member, counts[None, :], 0), axis=1)
    position = jnp.arange(ids.shape[0], dtype=jnp.int32) - start_row
    valid = (position < count_row).astype(jnp.float32)
    return (member.astype(jnp.float32), valid)


def sum_groups(local_mass):
    return 1.0 + lax.psum(local_mass, "dp")


def body(
    residual,
    ffn_gain,
    gate_weight,
    up_weight,
    down_weight,
    final_gain,
    head_weight,
    passage_ids,
    valid_counts,
):
    highest = lax.Precision.HIGHEST
    own_rows = residual.astype(jnp.float32)
    tok_rows = own_rows.shape[0]
    group_rows = tok_rows * lax.axis_size("mp")
    normed_in = (own_rows * rms_scale(own_rows) * ffn_gain).astype(jnp.bfloat16)
    gathered = lax.all_gather(normed_in, "mp", axis=0, tiled=True)
    offset = lax.axis_index("mp") * tok_rows
    placed = lax.dynamic_update_slice_in_dim(
        jnp.zeros((group_rows, own_rows.shape[1]), jnp.float32), own_rows, offset, 0
    )
    row_block = gathered
    gate_vals = jnp.dot(row_block, gate_weight, preferred_element_type=jnp.float32)
    up_vals = jnp.dot(row_block, up_weight, preferred_element_type=jnp.float32)
    activated = (jax.nn.silu(gate_vals) * up_vals).astype(jnp.bfloat16)
    hidden_all = lax.psum(
        jnp.dot(activated, down_weight, preferred_element_type=jnp.float32) + placed, "mp"
    )
    scale_all = rms_scale(hidden_all)
    normed_all = (hidden_all * scale_all * final_gain).astype(jnp.bfloat16)
    logits = jnp.dot(normed_all, head_weight, preferred_element_type=jnp.float32)
    hidden = lax.dynamic_slice_in_dim(hidden_all, offset, tok_rows, 0)
    scale = lax.dynamic_slice_in_dim(scale_all, offset, tok_rows, 0)
    member, valid = pool_masks(passage_ids[0], valid_counts[0])
    weights = jnp.log1p(jnp.maximum(logits, 0.0))
    powered = valid[:, None] * weights**4
    pooled_sum = lax.dot_general(member, powered, (((0,), (0,)), ((), ())), precision=highest)
    term_weights = (1.0 + pooled_sum) ** 0.25 - 1.0
    local_mass = jnp.sum(term_weights, axis=0)
    smooth = sum_groups(local_mass)
    total = lax.psum(jnp.sum(smooth), "mp")
    spread = lax.psum(jnp.sum(smooth * jnp.log(smooth)), "mp")
    entropy = jnp.log(total) - spread / total
    slope_mass = jnp.log(total) - jnp.log(smooth)
    factor = (1.0 + pooled_sum) ** (-0.75)
    row_factor = jnp.dot(member, factor, precision=highest)
    slope_logit = (
        valid[:, None]
        * weights**3
        * row_factor
        * slope_mass[None, :]
        / (1.0 + jnp.maximum(logits, 0.0))
    ).astype(jnp.bfloat16)
    row_block = slope_logit
    slope_normed = lax.psum_scatter(
        lax.dot_general(
            row_block, head_weight, (((1,), (1,)), ((), ())), preferred_element_type=jnp.float32
        ),
        "mp",
        scatter_dimension=0,
        tiled=True,
    )
    scaled_slope = slope_normed * final_gain
    grad_hidden = scale * scaled_slope - hidden * scale**3 * jnp.mean(
        scaled_slope * hidden, axis=-1, keepdims=True
    )
    return (term_weights, entropy, grad_hidden)


def solution(mesh):
    placed = (
        P(("dp", "mp"), None),
        P(),
        P(None, "mp"),
        P(None, "mp"),
        P("mp", None),
        P(),
        P(None, "mp"),
        P("dp", None),
        P("dp", None),
    )
    return jax.shard_map(
        body,
        mesh=mesh,
        in_specs=placed,
        out_specs=(P("dp", "mp"), P(), P(("dp", "mp"), None)),
        check_vma=False,
    )
```

profile of v0, /device:TPU:0, one launch (start us, length us, event | category | flops | bytes accessed | tf_op | source)
XLA Modules:
  0.0 332.3 jit_solution(6549865672109879377)
XLA Ops:
  7.2 0.0 all-gather.2.cloned.1.call-start
  7.2 1.1 fusion.12
  8.3 1.8 fusion.14
  10.1 0.0 all-gather.2.cloned.1.call-update
  10.1 0.0 all-reduce.3.cloned.1.call-start
  10.2 31.9 %all-gather.2.cloned.1.call-done = bf16[256,4096]{1,0:T(8,128)(2,1)} async-done(((bf16[32,4096]{1,0:T(8,128)(2,1)}), bf16[256,4096]{1,0:T(8,128)(2,1)}) %all-gather.2.cloned.1.call-update) | async-done | bytes 2097168 | tf_op jit(solution)/shard_map/all_gather | solution.py:42
  42.1 0.0 copy-start.4
  42.1 6.5 %fusion.26 = f32[256,1024]{1,0:T(8,128)S(1)} fusion(bf16[256,4096]{1,0:T(8,128)(2,1)} %all-gather.2.cloned.1.call-done, bf16[4096,1024]{1,0:T(8,128)(2,1)} %param.11), kind=kOutput, calls=%fused_computation.52 | convolution fusion | flops 2147483648 | bytes 11534336 | tf_op jit(solution)/shard_map/dot_general | solution.py:48
  48.6 0.0 copy-done.4
  48.6 0.0 copy-start
  48.6 0.0 copy-start.2
  48.6 0.0 copy-start.3
  48.6 12.5 %fusion.11 = f32[256,4096]{1,0:T(8,128)} fusion(bf16[1024,4096]{1,0:T(8,128)(2,1)} %param.13, bf16[256,4096]{1,0:T(8,128)(2,1)S(1)} %copy-done.4, bf16[4096,1024]{1,0:T(8,128)(2,1)} %param.12, f32[256,1024]{1,0:T(8,128)S(1)} %fusion.26), kind=kOutput, calls=%fused_computation.21 | convolution fusion | flops 4296540160 | bytes 24117248 | tf_op jit(solution)/shard_map/dot_general | solution.py:52
  61.1 0.0 copy-done
  61.1 0.0 copy-start.1
  61.1 1.9 fusion.15
  63.0 0.0 all-reduce.3.cloned.1.call-update
  63.1 0.2 reduce-scatter.2.cloned.1.call-start
  63.3 0.0 copy-done.2
  63.3 0.1 convert_reduce_fusion
  63.4 0.0 copy-done.3
  63.4 0.1 select_reduce_fusion.1
  63.5 95.8 %all-reduce.3.cloned.1.call-done = f32[256,4096]{1,0:T(8,128)} async-done(((f32[256,4096]{1,0:T(8,128)}), f32[256,4096]{1,0:T(8,128)}) %all-reduce.3.cloned.1.call-update) | async-done | bytes 4194320 | tf_op jit(solution)/shard_map/psum | solution.py:51
  159.3 2.5 multiply_reduce_fusion
  161.8 0.0 copy-done.1
  161.8 29.8 %convolution_maximum_fusion = f32[256,8192]{1,0:T(8,128)} fusion(bf16[4096,8192]{1,0:T(8,128)(2,1)} %param.15, f32[256,4096]{1,0:T(8,128)} %all-reduce.3.cloned.1.call-done, f32[4096]{0:T(1024)S(1)} %copy-done.1, f32[256]{0:T(256)S(1)} %add_rsqrt_fusion), kind=kOutput, calls=%fused_computation.4 | convolution fusion | flops 17185112064 | bytes 79709184 | tf_op jit(solution)/shard_map/dot_general | solution.py:56
  191.6 10.1 %fusion.25 = (f32[8192]{0:T(1024)S(1)}, f32[4,8192]{1,0:T(4,128)}, f32[4,8192]{1,0:T(4,128)S(1)}) fusion(f32[256,8192]{1,0:T(8,128)} %convolution_maximum_fusion, f32[256]{0:T(256)S(1)} %compare_convert_fusion, s32[256]{0:T(256)S(1)} %bitcast.16), kind=kOutput, calls=%fused_computation.51 | convolution fusion | flops 107045888 | bytes 8685568 | tf_op jit(solution)/shard_map/dot_general | solution.py:62
  201.7 16.2 %psum.29 = f32[8192]{0:T(1024)S(1)} all-reduce(f32[8192]{0:T(1024)S(1)} %get-tuple-element.11), channel_id=1, replica_groups=mesh['dp'=4,'mp'=8] {'dp'}, use_global_device_ids=true, to_apply=%region_7.8 | all-reduce | flops 8192 | bytes 65536 | tf_op jit(solution)/shard_map/psum | solution.py:23
  217.9 0.6 fusion.19
  218.5 14.5 %all-reduce = (f32[]{:T(128)}, f32[]{:T(128)}) all-reduce(f32[]{:T(128)} %get-tuple-element.4, f32[]{:T(128)} %get-tuple-element.3), channel_id=1, replica_groups=mesh['dp'=4,'mp'=8] {'mp'}, use_global_device_ids=true, to_apply=%region_9.10 | all-reduce | flops 2 | bytes 16 | tf_op jit(solution)/shard_map/psum | solution.py:66
  233.7 11.8 %fusion.2 = bf16[256,8192]{1,0:T(8,128)(2,1)} fusion(f32[256,8192]{1,0:T(8,128)} %convolution_maximum_fusion, f32[8192]{0:T(1024)S(1)} %log_subtract_fusion, f32[256]{0:T(256)S(1)} %compare_convert_fusion, f32[4,8192]{1,0:T(4,128)S(1)} %get-tuple-element.13, s32[256]{0:T(256)S(1)} %bitcast.17), kind=kOutput, calls=%fused_computation.7 | convolution fusion | flops 117441536 | bytes 12748800 | tf_op jit(solution)/shard_map/dot_general | solution.py:71
  245.5 29.1 %fusion.27 = f32[256,4096]{1,0:T(8,128)} fusion(bf16[256,8192]{1,0:T(8,128)(2,1)} %fusion.2, bf16[4096,8192]{1,0:T(8,128)(2,1)} %param.15), kind=kOutput, calls=%fused_computation.53 | convolution fusion | flops 17179869184 | bytes 75497472 | tf_op jit(solution)/shard_map/dot_general | solution.py:81
  274.6 0.0 reduce-scatter.2.cloned.1.call-update
  275.9 0.1 fusion.22
  276.0 45.1 %reduce-scatter.2.cloned.1.call-done = f32[32,4096]{1,0:T(8,128)} async-done(((f32[256,4096]{1,0:T(8,128)}), f32[32,4096]{1,0:T(8,128)}) %reduce-scatter.2.cloned.1.call-update) | async-done | bytes 524304 | tf_op jit(solution)/shard_map/reduce_scatter | solution.py:80
  321.1 1.4 multiply_reduce_fusion.1
  322.5 2.1 multiply_subtract_fusion
  (5 shorter events, 0.0 us)
Async XLA Ops:
  7.2 34.9 %all-gather.2.cloned.1.call-start = ((), (), s32[]{:S(2)}) async-start(), calls=%async_computation.1 | async-start | bytes 2359296 | tf_op jit(solution)/shard_map/all_gather | solution.py:42
  10.1 149.1 %all-reduce.3.cloned.1.call-start = ((), (), s32[]{:S(2)}) async-start(), calls=%async_computation.2 | async-start | bytes 8388608 | tf_op jit(solution)/shard_map/psum | solution.py:51
  42.1 6.5 %copy-start.4 = (bf16[256,4096]{1,0:T(8,128)(2,1)S(1)}, bf16[256,4096]{1,0:T(8,128)(2,1)}, u32[]{:S(2)}) copy-start(bf16[256,4096]{1,0:T(8,128)(2,1)} %all-gather.2.cloned.1.call-done) | copy-start | bytes 6291460
  48.6 12.5 %copy-start = (bf16[32,4096]{1,0:T(8,128)(2,1)S(1)}, bf16[32,4096]{1,0:T(8,128)(2,1)}, u32[]{:S(2)}) copy-start(bf16[32,4096]{1,0:T(8,128)(2,1)} %param.9) | copy-start | bytes 786436
  48.6 14.7 %copy-start.2 = (s32[1,256]{1,0:T(1,128)S(1)}, s32[1,256]{1,0:T(1,128)}, u32[]{:S(2)}) copy-start(s32[1,256]{1,0:T(1,128)} %param.16) | copy-start | bytes 3076
  48.6 14.8 %copy-start.3 = (s32[1,4]{1,0:T(1,128)S(1)}, s32[1,4]{1,0:T(1,128)}, u32[]{:S(2)}) copy-start(s32[1,4]{1,0:T(1,128)} %param.17) | copy-start | bytes 52
  61.1 100.7 %copy-start.1 = (f32[4096]{0:T(1024)S(1)}, f32[4096]{0:T(1024)}, u32[]{:S(2)}) copy-start(f32[4096]{0:T(1024)} %param.14) | copy-start | bytes 49156
  63.1 258.1 %reduce-scatter.2.cloned.1.call-start = ((), (), s32[]{:S(2)}) async-start(), calls=%async_computation.3 | async-start | bytes 4718592 | tf_op jit(solution)/shard_map/reduce_scatter | solution.py:80
Sparse Core Ops, SparseCore 0:
  10.3 31.7 all-gather.1
  63.2 96.0 all-reduce.2
  274.7 46.3 reduce-scatter.1
where the time goes:
time: 333 us; the launch traced here: 332 us
  waiting for transfers between devices  173 us (52%)
  matrix products  99.7 us (30%)
  blocking collectives  30.7 us (9%)
  between operations  17 us (5%)
  other arithmetic  11.8 us (4%)
    psum x1, waiting for transfers between devices, body(): lax.psum(jnp.dot(activated, down_weight, preferred_element_type=jnp.float...  95.8 us
    reduce_scatter x1, waiting for transfers between devices, body(): lax.psum_scatter(lax.dot_general(row_block, head_weight, (((1,), (1,)), (...  45.1 us
    all_gather x1, waiting for transfers between devices, body(): gathered = lax.all_gather(normed_in, 'mp', axis=0, tiled=True)  31.9 us
    dot_general x1, matrix products, body(): jnp.dot(normed_all, head_weight, preferred_element_type=jnp.float32)  29.8 us
    dot_general x1, matrix products, body(): lax.dot_general(row_block, head_weight, (((1,), (1,)), ((), ())), preferr...  29.1 us
    psum x1, blocking collectives, sum_groups(): return 1.0 + lax.psum(local_mass, 'dp')  16.2 us
    psum x1, blocking collectives, body(): total = lax.psum(jnp.sum(smooth), 'mp')  14.5 us
    dot_general x1, matrix products, body(): jnp.dot(activated, down_weight, preferred_element_type=jnp.float32) + placed  12.5 us
  transfers between devices with their start and end apart: 3, of which 3 were waited for; matrix products, arithmetic and copies ran while one was open for 0% of the time, Pallas kernels for 0%

commit v1 on v0

v1 whole, which is shorter than its diff:
```python
import functools

import jax
import jax.numpy as jnp
from jax import lax
from jax.experimental import pallas as pl
from jax.experimental.pallas import tpu as pltpu
from jax.sharding import PartitionSpec as P

MIB = 1024 * 1024
MESH = pl.DeviceIdType.MESH


def place():
    dp, me = lax.axis_index("dp"), lax.axis_index("mp")
    return dp, me, lax.div(me, 2), lax.rem(me, 2)


def greet(chips):
    dp, me, chip, core = place()
    barrier = pltpu.get_barrier_semaphore()
    pl.semaphore_signal(barrier, inc=1, device_id=(dp, chip * 2 + 1 - core), device_id_type=MESH)
    for k in range(1, chips):
        peer = lax.rem(chip + k, chips) * 2 + core
        pl.semaphore_signal(barrier, inc=1, device_id=(dp, peer), device_id_type=MESH)
    pl.semaphore_wait(barrier, chips)


def normed_rows(values, gain):
    scale = lax.rsqrt(jnp.mean(values * values, axis=-1, keepdims=True) + 1e-05)
    return (values * scale * gain).astype(jnp.bfloat16)


def gather_blocks(chips, own, out, local_sem, z_send, z_recv, c_send, c_recv):
    dp, me, chip, core = place()
    twin = chip * 2 + 1 - core
    sends = []
    for k in range(1, chips):
        peer = lax.rem(chip + k, chips) * 2 + core
        copy = pltpu.make_async_remote_copy(
            src_ref=own, dst_ref=out.at[me], send_sem=z_send.at[k - 1], recv_sem=z_recv.at[k - 1],
            device_id=(dp, peer), device_id_type=MESH,
        )
        copy.start()
        sends.append(copy)
    first = pltpu.make_async_remote_copy(
        src_ref=own, dst_ref=out.at[me], send_sem=c_send.at[0], recv_sem=c_recv.at[0],
        device_id=(dp, twin), device_id_type=MESH,
    )
    first.start()
    local = pltpu.make_async_copy(own, out.at[me], local_sem)
    local.start()
    passed = [first]
    for k in sorted(range(1, chips), key=lambda k: min(k, chips - k)):
        source = lax.rem(chip + chips - k, chips) * 2 + core
        sends[k - 1].wait_recv()
        onward = pltpu.make_async_remote_copy(
            src_ref=out.at[source], dst_ref=out.at[source], send_sem=c_send.at[k], recv_sem=c_recv.at[k],
            device_id=(dp, twin), device_id_type=MESH,
        )
        onward.start()
        passed.append(onward)
    local.wait()
    for copy in sends:
        copy.wait_send()
    for copy in passed:
        copy.wait()


def gather_sems(chips):
    dma = pltpu.SemaphoreType.DMA
    return [dma, dma((chips - 1,)), dma((chips - 1,)), dma((chips,)), dma((chips,))]


def norm_gather_kernel(chips, rows_ref, gain_ref, out, own, *sems):
    own[...] = normed_rows(rows_ref[...].astype(jnp.float32), gain_ref[...])
    greet(chips)
    gather_blocks(chips, own, out, *sems)


def norm_gather(residual, gain, size):
    rows, width = residual.shape
    chips = size // 2
    return pl.pallas_call(
        functools.partial(norm_gather_kernel, chips),
        out_shape=jax.ShapeDtypeStruct((size, rows, width), jnp.bfloat16),
        in_specs=[pl.BlockSpec(memory_space=pltpu.VMEM)] * 2,
        out_specs=pl.BlockSpec(memory_space=pl.ANY),
        scratch_shapes=[pltpu.VMEM((rows, width), jnp.bfloat16)] + gather_sems(chips),
        compiler_params=pltpu.CompilerParams(
            collective_id=0, has_side_effects=True, vmem_limit_bytes=24 * MIB
        ),
    )(residual, gain.reshape(1, width))


def sum_norm_gather_kernel(
    chips, part, rows_ref, gain_ref, hidden_ref, out, own, pair, outgo, arrived,
    p_send, p_recv, s_send, s_recv, *sems,
):
    dp, me, chip, core = place()
    twin = chip * 2 + 1 - core
    greet(chips)
    order = list(range(1, chips)) + [0]
    swaps = {}
    for k in order:
        peer = lax.rem(chip + k, chips)
        swaps[k] = pltpu.make_async_remote_copy(
            src_ref=part.at[peer * 2 + 1 - core], dst_ref=pair.at[k],
            send_sem=p_send.at[k], recv_sem=p_recv.at[k],
            device_id=(dp, twin), device_id_type=MESH,
        )
        swaps[k].start()
    sends = []
    for k in order:
        peer = lax.rem(chip + k, chips)
        swaps[k].wait_recv()
        both = part[peer * 2 + core] + pair[k]
        if k == 0:
            hidden_ref[...] = both + rows_ref[...].astype(jnp.float32)
        else:
            outgo[k - 1] = both.astype(jnp.bfloat16)
            copy = pltpu.make_async_remote_copy(
                src_ref=outgo.at[k - 1], dst_ref=arrived.at[k - 1],
                send_sem=s_send.at[k - 1], recv_sem=s_recv.at[k - 1],
                device_id=(dp, peer * 2 + core), device_id_type=MESH,
            )
            copy.start()
            sends.append(copy)
    for copy in sends:
        copy.wait_recv()
    hidden = hidden_ref[...]
    for k in range(chips - 1):
        hidden = hidden + arrived[k].astype(jnp.float32)
    hidden_ref[...] = hidden
    own[...] = normed_rows(hidden, gain_ref[...])
    gather_blocks(chips, own, out, *sems)
    for copy in sends:
        copy.wait_send()
    for k in order:
        swaps[k].wait_send()


def sum_norm_gather(part, residual, gain, size):
    rows, width = residual.shape
    chips = size // 2
    dma = pltpu.SemaphoreType.DMA
    return pl.pallas_call(
        functools.partial(sum_norm_gather_kernel, chips),
        out_shape=(
            jax.ShapeDtypeStruct((rows, width), jnp.float32),
            jax.ShapeDtypeStruct((size, rows, width), jnp.bfloat16),
        ),
        in_specs=[pl.BlockSpec(memory_space=pltpu.VMEM)] * 3,
        out_specs=(pl.BlockSpec(memory_space=pltpu.VMEM), pl.BlockSpec(memory_space=pl.ANY)),
        scratch_shapes=[
            pltpu.VMEM((rows, width), jnp.bfloat16),
            pltpu.VMEM((chips, rows, width), jnp.float32),
            pltpu.VMEM((chips - 1, rows, width), jnp.bfloat16),
            pltpu.VMEM((chips - 1, rows, width), jnp.bfloat16),
            dma((chips,)), dma((chips,)), dma((chips - 1,)), dma((chips - 1,)),
        ] + gather_sems(chips),
        compiler_params=pltpu.CompilerParams(
            collective_id=1, has_side_effects=True, vmem_limit_bytes=32 * MIB
        ),
    )(part.reshape(size, rows, width), residual, gain.reshape(1, width))


def slope_kernel(
    chips, steps, deep, slope, head, hidden_ref, gain_ref, grad_ref, total, part, pair, outgo, arrived,
    p_send, p_recv, s_send, s_recv,
):
    dp, me, chip, core = place()
    twin = chip * 2 + 1 - core
    rows = hidden_ref.shape[0]
    wide = head.shape[0]
    step = pl.program_id(0)

    @pl.when(step == 0)
    def _():
        greet(chips)

    total[...] = jnp.zeros_like(total)

    @pl.loop(0, slope.shape[1] // deep)
    def _(at):
        span = pl.ds(pl.multiple_of(at * deep, deep), deep)
        total[...] += lax.dot_general(
            slope[:, span], head[:, span], (((1,), (1,)), ((), ())),
            preferred_element_type=jnp.float32,
        )

    for z in range(chips):
        for c in range(2):
            block = z * 2 + c
            part[step, c, z] = total[block * rows:(block + 1) * rows, :]

    def swap(at):
        return pltpu.make_async_remote_copy(
            src_ref=part.at[at, 1 - core], dst_ref=pair.at[at],
            send_sem=p_send.at[at], recv_sem=p_recv.at[at],
            device_id=(dp, twin), device_id_type=MESH,
        )

    def send(at, k):
        peer = lax.rem(chip + k, chips)
        return pltpu.make_async_remote_copy(
            src_ref=outgo.at[at, k - 1], dst_ref=arrived.at[at, k - 1],
            send_sem=s_send.at[at, k - 1], recv_sem=s_recv.at[at, k - 1],
            device_id=(dp, peer * 2 + core), device_id_type=MESH,
        )

    def forward(at):
        swap(at).wait_recv()
        for k in range(1, chips):
            peer = lax.rem(chip + k, chips)
            outgo[at, k - 1] = (part[at, core, peer] + pair[at, peer]).astype(jnp.bfloat16)
            send(at, k).start()

    swap(step).start()

    @pl.when(step > 0)
    def _():
        forward(step - 1)

    @pl.when(step == steps - 1)
    def _():
        forward(steps - 1)
        hidden = hidden_ref[...]
        scale = lax.rsqrt(jnp.mean(hidden * hidden, axis=-1, keepdims=True) + 1e-05)
        inner = jnp.zeros((rows, 1), jnp.float32)
        for at in range(steps):
            span = slice(at * wide, (at + 1) * wide)
            value = part[at, core, chip] + pair[at, chip]
            for k in range(1, chips):
                send(at, k).wait_recv()
                value = value + arrived[at, k - 1].astype(jnp.float32)
            value = value * gain_ref[:, span]
            grad_ref[:, span] = value
            inner = inner + jnp.sum(value * hidden_ref[:, span], axis=-1, keepdims=True)
        inner = inner / (steps * wide)
        grad_ref[...] = scale * grad_ref[...] - hidden_ref[...] * (scale * scale * scale * inner)
        for at in range(steps):
            swap(at).wait_send()
            for k in range(1, chips):
                send(at, k).wait_send()


def slope_grad(slope, head, hidden, gain, size):
    rows, width = hidden.shape
    group, vocab = slope.shape
    chips = size // 2
    wide = min(512, width)
    steps = width // wide
    deep = min(2048, vocab)
    dma = pltpu.SemaphoreType.DMA
    return pl.pallas_call(
        functools.partial(slope_kernel, chips, steps, deep),
        grid=(steps,),
        out_shape=jax.ShapeDtypeStruct((rows, width), jnp.float32),
        in_specs=[
            pl.BlockSpec((group, vocab), lambda i: (0, 0)),
            pl.BlockSpec((wide, vocab), lambda i: (i, 0)),
            pl.BlockSpec((rows, width), lambda i: (0, 0)),
            pl.BlockSpec((1, width), lambda i: (0, 0)),
        ],
        out_specs=pl.BlockSpec((rows, width), lambda i: (0, 0)),
        scratch_shapes=[
            pltpu.VMEM((group, wide), jnp.float32),
            pltpu.VMEM((steps, 2, chips, rows, wide), jnp.float32),
            pltpu.VMEM((steps, chips, rows, wide), jnp.float32),
            pltpu.VMEM((steps, chips - 1, rows, wide), jnp.bfloat16),
            pltpu.VMEM((steps, chips - 1, rows, wide), jnp.bfloat16),
            dma((steps,)), dma((steps,)), dma((steps, chips - 1)), dma((steps, chips - 1)),
        ],
        compiler_params=pltpu.CompilerParams(
            collective_id=2, has_side_effects=True, vmem_limit_bytes=48 * MIB
        ),
    )(slope, head, hidden, gain.reshape(1, width))


def rms_scale(values):
    return lax.rsqrt(jnp.mean(values * values, axis=-1, keepdims=True) + 1e-05)


def pool_masks(ids, counts):
    slots = jnp.arange(counts.shape[0], dtype=jnp.int32)
    member = ids[:, None] == slots[None, :]
    starts = jnp.sum((ids[:, None] < slots[None, :]).astype(jnp.int32), axis=0)
    start_row = jnp.sum(jnp.where(member, starts[None, :], 0), axis=1)
    count_row = jnp.sum(jnp.where(member, counts[None, :], 0), axis=1)
    position = jnp.arange(ids.shape[0], dtype=jnp.int32) - start_row
    valid = (position < count_row).astype(jnp.float32)
    return (member.astype(jnp.float32), valid)


def body(
    line,
    residual,
    ffn_gain,
    gate_weight,
    up_weight,
    down_weight,
    final_gain,
    head_weight,
    passage_ids,
    valid_counts,
):
    highest = lax.Precision.HIGHEST
    tok_rows, width = residual.shape
    size = lax.axis_size("mp")
    group_rows = tok_rows * size
    if line:
        gathered = norm_gather(residual, ffn_gain, size).reshape(group_rows, width)
    else:
        own_rows = residual.astype(jnp.float32)
        normed_in = (own_rows * rms_scale(own_rows) * ffn_gain).astype(jnp.bfloat16)
        gathered = lax.all_gather(normed_in, "mp", axis=0, tiled=True)
    gate_vals = jnp.dot(gathered, gate_weight, preferred_element_type=jnp.float32)
    up_vals = jnp.dot(gathered, up_weight, preferred_element_type=jnp.float32)
    activated = (jax.nn.silu(gate_vals) * up_vals).astype(jnp.bfloat16)
    part = jnp.dot(activated, down_weight, preferred_element_type=jnp.float32)
    if line:
        hidden, normed_all = sum_norm_gather(part, residual, final_gain, size)
        normed_all = normed_all.reshape(group_rows, width)
    else:
        hidden = own_rows + lax.psum_scatter(part, "mp", scatter_dimension=0, tiled=True)
        normed = (hidden * rms_scale(hidden) * final_gain).astype(jnp.bfloat16)
        normed_all = lax.all_gather(normed, "mp", axis=0, tiled=True)
    logits = jnp.dot(normed_all, head_weight, preferred_element_type=jnp.float32)
    member, valid = pool_masks(passage_ids[0], valid_counts[0])
    weights = jnp.log1p(jnp.maximum(logits, 0.0))
    powered = valid[:, None] * weights**4
    pooled_sum = lax.dot_general(member, powered, (((0,), (0,)), ((), ())), precision=highest)
    term_weights = (1.0 + pooled_sum) ** 0.25 - 1.0
    local_mass = jnp.sum(term_weights, axis=0)
    entries = local_mass.shape[0] * size
    smooth = 1.0 + lax.psum(local_mass, "dp")
    total = entries + lax.psum(jnp.sum(local_mass), ("dp", "mp"))
    slope_mass = jnp.log(total) - jnp.log(smooth)
    factor = (1.0 + pooled_sum) ** (-0.75)
    row_factor = jnp.dot(member, factor, precision=highest)
    slope_logit = (
        valid[:, None]
        * weights**3
        * row_factor
        * slope_mass[None, :]
        / (1.0 + jnp.maximum(logits, 0.0))
    ).astype(jnp.bfloat16)
    if line:
        grad_hidden = slope_grad(slope_logit, head_weight, hidden, final_gain, size)
    else:
        slope_normed = lax.psum_scatter(
            lax.dot_general(
                slope_logit, head_weight, (((1,), (1,)), ((), ())), preferred_element_type=jnp.float32
            ),
            "mp",
            scatter_dimension=0,
            tiled=True,
        )
        scale = rms_scale(hidden)
        scaled_slope = slope_normed * final_gain
        grad_hidden = scale * scaled_slope - hidden * scale**3 * jnp.mean(
            scaled_slope * hidden, axis=-1, keepdims=True
        )
    spread = lax.psum(jnp.sum(smooth * jnp.log(smooth)), "mp")
    entropy = jnp.log(total) - spread / total
    return (term_weights, entropy, grad_hidden)


def solution(mesh):
    placed = (
        P(("dp", "mp"), None),
        P(),
        P(None, "mp"),
        P(None, "mp"),
        P("mp", None),
        P(),
        P(None, "mp"),
        P("dp", None),
        P("dp", None),
    )
    line = mesh.shape["mp"] == 8
    return jax.shard_map(
        functools.partial(body, line),
        mesh=mesh,
        in_specs=placed,
        out_specs=(P("dp", "mp"), P(), P(("dp", "mp"), None)),
        check_vma=False,
    )
```

time: 333 us -> 275 us (0.83)
  waiting for transfers between devices: 173 us -> 0 us
  Pallas kernels: 0 us -> 115 us
  blocking collectives: 30.7 us -> 77 us
  matrix products: 99.7 us -> 70.6 us
  between operations: 17 us -> 3.21 us
  other arithmetic: 11.8 us -> 2.19 us
  local copies, waits for them, and re-layouts: 0.03 us -> 6.05 us
    pallas_call x0 -> x3, Pallas kernels: none -> 115 us  [the longest x1 52.2 us: sum_norm_gather(): pl.pallas_call(functools.partial(sum_norm_gather_kernel, chips), out_shap...]
    psum x1 -> x0, waiting for transfers between devices: 95.8 us -> none  [body(): lax.psum(jnp.dot(activated, down_weight, preferred_element_type=jnp.float...]
    psum x2 -> x3, blocking collectives: 30.7 us -> 77 us  [the longest x1 46.2 us: body(): total = entries + lax.psum(jnp.sum(local_mass), ('dp', 'mp'))]
    reduce_scatter x1 -> x0, waiting for transfers between devices: 45.1 us -> none  [body(): lax.psum_scatter(lax.dot_general(row_block, head_weight, (((1,), (1,)), (...]
    all_gather x1 -> x0, waiting for transfers between devices: 31.9 us -> none  [body(): gathered = lax.all_gather(normed_in, 'mp', axis=0, tiled=True)]
    dot_general x3 -> x2, matrix products: 48.1 us -> 18.3 us  [the longest x1 12.5 us: body(): part = jnp.dot(activated, down_weight, preferred_element_type=jnp.float32)]
    unnamed x10 -> x15, local copies, waits for them, and re-layouts: 0.03 us -> 6.05 us
    reduce_sum x4 -> x0, other arithmetic: 5.64 us -> none  [the longest x2 3.66 us: rms_scale(): return lax.rsqrt(jnp.mean(values * values, axis=-1, keepdims=True) + 1e-05)]
  transfers between devices with their start and end apart: 3 -> 0, of which waited for: 3 -> 0; matrix products, arithmetic and copies ran while one was open for 0% -> 0% of each run, Pallas kernels for 0% -> 0%
where the time goes in v1:
time: 275 us; the launch traced here: 274 us
  Pallas kernels  115 us (42%)
  blocking collectives  77 us (28%)
  matrix products  70.6 us (26%)
  local copies, waits for them, and re-layouts  6.05 us (2%)
  between operations  3.21 us (1%)
    pallas_call x1, Pallas kernels, sum_norm_gather(): pl.pallas_call(functools.partial(sum_norm_gather_kernel, chips), out_shap...  52.2 us
    psum x1, blocking collectives, body(): total = entries + lax.psum(jnp.sum(local_mass), ('dp', 'mp'))  46.2 us
    pallas_call x1, Pallas kernels, slope_grad(): pl.pallas_call(functools.partial(slope_kernel, chips, steps, deep), grid=...  38.3 us
    dot_general x1, matrix products, body(): jnp.dot(normed_all, head_weight, preferred_element_type=jnp.float32)  31.1 us
    pallas_call x1, Pallas kernels, norm_gather(): pl.pallas_call(functools.partial(norm_gather_kernel, chips), out_shape=ja...  24.9 us
    psum x1, blocking collectives, body(): smooth = 1.0 + lax.psum(local_mass, 'dp')  16.3 us
    psum x1, blocking collectives, body(): spread = lax.psum(jnp.sum(smooth * jnp.log(smooth)), 'mp')  14.4 us
    dot_general x1, matrix products, body(): part = jnp.dot(activated, down_weight, preferred_element_type=jnp.float32)  12.5 us

profile of v1, /device:TPU:0, one launch (start us, length us, event | category | flops | bytes accessed | tf_op | source)
XLA Modules:
  0.0 274.3 jit_solution(3574967886463633779)
XLA Ops:
  0.6 0.8 convert_reduce_fusion
  1.4 0.8 select_reduce_fusion.1
  2.2 0.0 copy-start.1
  2.2 0.9 copy-done.1
  3.2 0.0 copy-start.4
  3.2 0.7 copy-done.4
  3.9 24.9 %shard_map.112 = bf16[8,32,4096]{2,1,0:T(8,128)(2,1)S(1)} custom-call(bf16[32,4096]{1,0:T(8,128)(2,1)S(1)} %copy-done.1, f32[1,4096]{1,0:T(1,128)S(1)} %bitcast.19), custom_call_target="tpu_custom_call" | custom-call | tf_op jit(solution)/shard_map/pallas_call | solution.py:84
  28.8 5.8 %fusion.19 = f32[256,1024]{1,0:T(8,128)S(1)} fusion(bf16[256,4096]{1,0:T(8,128)(2,1)S(1)} %bitcast.15, bf16[4096,1024]{1,0:T(8,128)(2,1)} %param.11), kind=kOutput, calls=%fused_computation.33 | convolution fusion | flops 2147483648 | bytes 11534336 | tf_op jit(solution)/shard_map/dot_general | solution.py:318
  34.6 0.0 copy-start.2
  34.6 0.0 copy-start.3
  34.6 12.5 %fusion.9 = f32[256,4096]{1,0:T(8,128)} fusion(bf16[1024,4096]{1,0:T(8,128)(2,1)} %param.13, bf16[256,4096]{1,0:T(8,128)(2,1)S(1)} %bitcast.16, bf16[4096,1024]{1,0:T(8,128)(2,1)} %param.12, f32[256,1024]{1,0:T(8,128)S(1)} %fusion.19), kind=kOutput, calls=%fused_computation.14 | convolution fusion | flops 4296540160 | bytes 24117248 | tf_op jit(solution)/shard_map/dot_general | solution.py:321
  47.1 0.0 copy-done.2
  47.1 0.0 copy-done.3
  47.1 0.0 copy-start
  47.1 2.2 copy-done
  49.3 52.2 %shard_map.113 = (f32[32,4096]{1,0:T(8,128)S(1)}, bf16[8,32,4096]{2,1,0:T(8,128)(2,1)S(1)}) custom-call(f32[8,32,4096]{2,1,0:T(8,128)S(1)} %bitcast.14, bf16[32,4096]{1,0:T(8,128)(2,1)S(1)} %copy-done.2, f32[1,4096]{1,0:T(1,128)S(1)} %bitcast.17), custom_call_target="tpu_custom_call" | custom-call | tf_op jit(solution)/shard_map/pallas_call | solution.py:147
  101.5 0.0 copy-start.5
  101.5 1.4 copy-done.5
  102.9 0.0 copy-start.6
  102.9 31.1 %convolution_maximum_fusion = f32[256,8192]{1,0:T(8,128)} fusion(bf16[256,4096]{1,0:T(8,128)(2,1)} %bitcast.20, bf16[4096,8192]{1,0:T(8,128)(2,1)} %head.1), kind=kOutput, calls=%fused_computation.4 | convolution fusion | flops 17181966336 | bytes 77594624 | tf_op jit(solution)/shard_map/dot_general | solution.py:329
  133.9 0.0 copy-done.6
  133.9 10.7 %fusion.18 = (f32[8192]{0:T(1024)S(1)}, f32[]{:T(128)}, f32[4,8192]{1,0:T(4,128)}, f32[4,8192]{1,0:T(4,128)S(1)}) fusion(f32[256,8192]{1,0:T(8,128)} %convolution_maximum_fusion, f32[256]{0:T(256)S(1)} %compare_convert_fusion, s32[256]{0:T(256)S(1)} %bitcast.23), kind=kOutput, calls=%fused_computation.32 | convolution fusion | flops 107078656 | bytes 8685572 | tf_op jit(solution)/shard_map/dot_general | solution.py:333
  144.6 46.2 %psum.21 = f32[]{:T(128)} all-reduce(f32[]{:T(128)} %get-tuple-element.8), channel_id=1, replica_groups=mesh['dp'=4,'mp'=8] {'dp','mp'}, use_global_device_ids=true, to_apply=%region_4.5 | all-reduce | flops 1 | bytes 8 | tf_op jit(solution)/shard_map/psum | solution.py:338
  191.5 16.3 %psum.22 = f32[8192]{0:T(1024)S(1)} all-reduce(f32[8192]{0:T(1024)S(1)} %get-tuple-element.7), channel_id=1, replica_groups=mesh['dp'=4,'mp'=8] {'dp'}, use_global_device_ids=true, to_apply=%region_6.7 | all-reduce | flops 8192 | bytes 65536 | tf_op jit(solution)/shard_map/psum | solution.py:337
  207.8 0.6 log_subtract_fusion
  208.5 14.4 %psum.23 = f32[]{:T(128)} all-reduce(f32[]{:T(128)} %get-tuple-element.13), channel_id=1, replica_groups=mesh['dp'=4,'mp'=8] {'mp'}, use_global_device_ids=true, to_apply=%region_8.9 | all-reduce | flops 1 | bytes 8 | tf_op jit(solution)/shard_map/psum | solution.py:365
  223.6 10.5 %fusion.2.slope = bf16[256,8192]{1,0:T(8,128)(2,1)S(1)} fusion(f32[256,8192]{1,0:T(8,128)} %convolution_maximum_fusion, f32[8192]{0:T(1024)S(1)} %get-tuple-element.12, f32[256]{0:T(256)S(1)} %compare_convert_fusion, f32[4,8192]{1,0:T(4,128)S(1)} %get-tuple-element.14, s32[256]{0:T(256)S(1)} %bitcast.24), kind=kOutput, calls=%fused_computation.7 | convolution fusion | flops 117441536 | bytes 12748800 | tf_op jit(solution)/shard_map/dot_general | solution.py:341
  234.1 38.3 %shard_map.114 = f32[32,4096]{1,0:T(8,128)S(1)} custom-call(bf16[256,8192]{1,0:T(8,128)(2,1)S(1)} %fusion.2.slope, bf16[4096,8192]{1,0:T(8,128)(2,1)} %head.1, f32[32,4096]{1,0:T(8,128)S(1)} %get-tuple-element.6.hidden_ref, f32[1,4096]{1,0:T(1,128)S(1)} %bitcast.18), custom_call_target="tpu_custom_call" | custom-call | tf_op jit(solution)/shard_map/pallas_call | solution.py:256
  272.4 0.8 copy.13
  (1 shorter events, 0.0 us)
Async XLA Ops:
  2.2 1.0 copy-start.1
  3.2 0.7 copy-start.4
  34.6 12.5 %copy-start.2 = (bf16[32,4096]{1,0:T(8,128)(2,1)S(1)}, bf16[32,4096]{1,0:T(8,128)(2,1)}, u32[]{:S(2)}) copy-start(bf16[32,4096]{1,0:T(8,128)(2,1)} %rows_ref.3) | copy-start | bytes 786436
  34.6 12.5 %copy-start.3 = (f32[4096]{0:T(1024)S(1)}, f32[4096]{0:T(1024)}, u32[]{:S(2)}) copy-start(f32[4096]{0:T(1024)} %param.14) | copy-start | bytes 49156
  47.1 2.2 copy-start
  101.5 1.4 copy-start.5
  102.9 31.1 %copy-start.6 = (s32[1,256]{1,0:T(1,128)S(1)}, s32[1,256]{1,0:T(1,128)}, u32[]{:S(2)}) copy-start(s32[1,256]{1,0:T(1,128)} %param.16) | copy-start | bytes 3076

commit v2 on v1

--- a/solution.py
+++ b/solution.py
@@ -276,6 +276,50 @@
             collective_id=2, has_side_effects=True, vmem_limit_bytes=48 * MIB
         ),
     )(slope, head, hidden, gain.reshape(1, width))
+
+
+def all_sum_kernel(axis, size, own, out, slots, sends, recvs):
+    dp, mp = lax.axis_index("dp"), lax.axis_index("mp")
+    me = lax.axis_index(axis)
+
+    def device(k):
+        peer = lax.rem(me + k, size)
+        return (peer, mp) if axis == "dp" else (dp, peer)
+
+    slots[me] = own[...]
+    barrier = pltpu.get_barrier_semaphore()
+    for k in range(1, size):
+        pl.semaphore_signal(barrier, inc=1, device_id=device(k), device_id_type=MESH)
+    pl.semaphore_wait(barrier, size - 1)
+    copies = []
+    for k in range(1, size):
+        copy = pltpu.make_async_remote_copy(
+            src_ref=own, dst_ref=slots.at[me], send_sem=sends.at[k - 1], recv_sem=recvs.at[k - 1],
+            device_id=device(k), device_id_type=MESH,
+        )
+        copy.start()
+        copies.append(copy)
+    for copy in copies:
+        copy.wait()
+    total = slots[0]
+    for at in range(1, size):
+        total = total + slots[at]
+    out[...] = total
+
+
+def all_sum(values, axis, number):
+    size = lax.axis_size(axis)
+    dma = pltpu.SemaphoreType.DMA
+    return pl.pallas_call(
+        functools.partial(all_sum_kernel, axis, size),
+        out_shape=jax.ShapeDtypeStruct(values.shape, jnp.float32),
+        in_specs=[pl.BlockSpec(memory_space=pltpu.VMEM)],
+        out_specs=pl.BlockSpec(memory_space=pltpu.VMEM),
+        scratch_shapes=[
+            pltpu.VMEM((size,) + values.shape, jnp.float32), dma((size - 1,)), dma((size - 1,)),
+        ],
+        compiler_params=pltpu.CompilerParams(collective_id=number, has_side_effects=True),
+    )(values)
 
 
 def rms_scale(values):
@@ -333,9 +377,15 @@
     pooled_sum = lax.dot_general(member, powered, (((0,), (0,)), ((), ())), precision=highest)
     term_weights = (1.0 + pooled_sum) ** 0.25 - 1.0
     local_mass = jnp.sum(term_weights, axis=0)
-    entries = local_mass.shape[0] * size
-    smooth = 1.0 + lax.psum(local_mass, "dp")
-    total = entries + lax.psum(jnp.sum(local_mass), ("dp", "mp"))
+    if line:
+        smooth = 1.0 + all_sum(local_mass.reshape(-1, 128), "dp", 3)
+        tiles = smooth.reshape(-1, 8, 128)
+        sums = jnp.stack([jnp.sum(tiles, axis=0), jnp.sum(tiles * jnp.log(tiles), axis=0)])
+        total, spread = jnp.sum(all_sum(sums, "mp", 4), axis=(1, 2))
+        smooth = smooth.reshape(-1)
+    else:
+        smooth = 1.0 + lax.psum(local_mass, "dp")
+        total, spread = lax.psum((jnp.sum(smooth), jnp.sum(smooth * jnp.log(smooth))), "mp")
     slope_mass = jnp.log(total) - jnp.log(smooth)
     factor = (1.0 + pooled_sum) ** (-0.75)
     row_factor = jnp.dot(member, factor, precision=highest)
@@ -362,7 +412,6 @@
         grad_hidden = scale * scaled_slope - hidden * scale**3 * jnp.mean(
             scaled_slope * hidden, axis=-1, keepdims=True
         )
-    spread = lax.psum(jnp.sum(smooth * jnp.log(smooth)), "mp")
     entropy = jnp.log(total) - spread / total
     return (term_weights, entropy, grad_hidden)
 

time: 275 us -> 222 us (0.81)
  blocking collectives: 77 us -> 0 us
  Pallas kernels: 115 us -> 137 us
    psum x3 -> x0, blocking collectives: 77 us -> none  [the longest x1 46.2 us: body(): total = entries + lax.psum(jnp.sum(local_mass), ('dp', 'mp'))]
    pallas_call x0 -> x2, Pallas kernels: none -> 20.3 us  [all_sum(): pl.pallas_call(functools.partial(all_sum_kernel, axis, size), out_shape=j...]
    unnamed x15 -> x13, local copies, waits for them, and re-layouts: 6.05 us -> 4.66 us
where the time goes in v2:
time: 222 us; the launch traced here: 221 us
  Pallas kernels  137 us (62%)
  matrix products  70.4 us (32%)
  local copies, waits for them, and re-layouts  5.24 us (2%)
  other arithmetic  4.52 us (2%)
  between operations  3.87 us (2%)
    pallas_call x1, Pallas kernels, sum_norm_gather(): pl.pallas_call(functools.partial(sum_norm_gather_kernel, chips), out_shap...  52.2 us
    pallas_call x1, Pallas kernels, slope_grad(): pl.pallas_call(functools.partial(slope_kernel, chips, steps, deep), grid=...  39.7 us
    dot_general x1, matrix products, body(): jnp.dot(normed_all, head_weight, preferred_element_type=jnp.float32)  29.7 us
    pallas_call x1, Pallas kernels, norm_gather(): pl.pallas_call(functools.partial(norm_gather_kernel, chips), out_shape=ja...  24.9 us
    pallas_call x2, Pallas kernels, all_sum(): pl.pallas_call(functools.partial(all_sum_kernel, axis, size), out_shape=j...  20.3 us
    dot_general x1, matrix products, body(): part = jnp.dot(activated, down_weight, preferred_element_type=jnp.float32)  12.8 us
    dot_general x1, matrix products, body(): lax.dot_general(member, powered, (((0,), (0,)), ((), ())), precision=high...  10.7 us
    dot_general x1, matrix products, body(): row_factor = jnp.dot(member, factor, precision=highest)  10.5 us

profile of v2, /device:TPU:0, one launch (start us, length us, event | category | flops | bytes accessed | tf_op | source)
XLA Modules:
  0.0 221.0 jit_solution(14141339621427243624)
XLA Ops:
  0.6 0.8 convert_reduce_fusion
  1.4 0.8 select_reduce_fusion.1
  2.2 0.0 copy-start.1
  2.2 0.9 copy-done.1
  3.2 0.0 copy-start.4
  3.2 0.7 copy-done.4
  3.9 24.9 %shard_map.112 = bf16[8,32,4096]{2,1,0:T(8,128)(2,1)S(1)} custom-call(bf16[32,4096]{1,0:T(8,128)(2,1)S(1)} %copy-done.1, f32[1,4096]{1,0:T(1,128)S(1)} %bitcast.29), custom_call_target="tpu_custom_call" | custom-call | tf_op jit(solution)/shard_map/pallas_call | solution.py:84
  28.8 6.8 %fusion.20 = f32[256,1024]{1,0:T(8,128)} fusion(bf16[256,4096]{1,0:T(8,128)(2,1)S(1)} %bitcast.25, bf16[4096,1024]{1,0:T(8,128)(2,1)} %param.11), kind=kOutput, calls=%fused_computation.36 | convolution fusion | flops 2147483648 | bytes 11534336 | tf_op jit(solution)/shard_map/dot_general | solution.py:362
  35.5 0.0 copy-start.2
  35.5 0.0 copy-start.3
  35.5 12.8 %fusion.9 = f32[256,4096]{1,0:T(8,128)} fusion(bf16[1024,4096]{1,0:T(8,128)(2,1)} %param.13, bf16[256,4096]{1,0:T(8,128)(2,1)S(1)} %bitcast.26, bf16[4096,1024]{1,0:T(8,128)(2,1)} %param.12, f32[256,1024]{1,0:T(8,128)} %fusion.20), kind=kOutput, calls=%fused_computation.14 | convolution fusion | flops 4296540160 | bytes 24117248 | tf_op jit(solution)/shard_map/dot_general | solution.py:365
  48.3 0.0 copy-done.2
  48.3 0.0 copy-done.3
  48.3 0.0 copy-start
  48.3 2.2 copy-done
  50.5 52.2 %shard_map.113 = (f32[32,4096]{1,0:T(8,128)S(1)}, bf16[8,32,4096]{2,1,0:T(8,128)(2,1)S(1)}) custom-call(f32[8,32,4096]{2,1,0:T(8,128)S(1)} %bitcast.24, bf16[32,4096]{1,0:T(8,128)(2,1)S(1)} %copy-done.2, f32[1,4096]{1,0:T(1,128)S(1)} %bitcast.27), custom_call_target="tpu_custom_call" | custom-call | tf_op jit(solution)/shard_map/pallas_call | solution.py:147
  102.7 0.0 copy-start.5
  102.7 29.7 %convolution_maximum_fusion = f32[256,8192]{1,0:T(8,128)} fusion(bf16[256,4096]{1,0:T(8,128)(2,1)S(1)} %bitcast.30, bf16[4096,8192]{1,0:T(8,128)(2,1)} %head.1), kind=kOutput, calls=%fused_computation.4 | convolution fusion | flops 17181966336 | bytes 77594624 | tf_op jit(solution)/shard_map/dot_general | solution.py:373
  132.4 0.0 copy-done.5
  132.4 10.7 %fusion.18 = (f32[8192]{0:T(1024)}, f32[4,8192]{1,0:T(4,128)}, f32[4,8192]{1,0:T(4,128)S(1)}) fusion(f32[256,8192]{1,0:T(8,128)} %convolution_maximum_fusion, f32[256]{0:T(256)S(1)} %compare_convert_fusion, s32[256]{0:T(256)S(1)} %bitcast.36), kind=kOutput, calls=%fused_computation.34 | convolution fusion | flops 107045888 | bytes 8685568 | tf_op jit(solution)/shard_map/dot_general | solution.py:377
  143.0 6.8 %shard_map.114 = f32[64,128]{1,0:T(8,128)} custom-call(f32[64,128]{1,0:T(8,128)} %bitcast.31), custom_call_target="tpu_custom_call" | custom-call | tf_op jit(solution)/shard_map/pallas_call | solution.py:313
  149.8 0.8 bitcast_reduce_fusion
  150.6 0.6 pad_maximum_fusion.own
  151.2 13.5 %shard_map.115 = f32[2,8,128]{2,1,0:T(8,128)} custom-call(f32[2,8,128]{2,1,0:T(8,128)} %pad_maximum_fusion.own), custom_call_target="tpu_custom_call" | custom-call | tf_op jit(solution)/shard_map/pallas_call | solution.py:313
  164.7 0.8 reduce_sum.69
  165.5 0.6 fusion.19
  168.1 0.8 subtract_bitcast_fusion
  168.9 10.5 %fusion.2.slope = bf16[256,8192]{1,0:T(8,128)(2,1)S(1)} fusion(f32[256,8192]{1,0:T(8,128)} %convolution_maximum_fusion, f32[8192]{0:T(1024)S(1)} %subtract_bitcast_fusion, f32[256]{0:T(256)S(1)} %compare_convert_fusion, f32[4,8192]{1,0:T(4,128)S(1)} %get-tuple-element.15, s32[256]{0:T(256)S(1)} %bitcast.37), kind=kOutput, calls=%fused_computation.7 | convolution fusion | flops 117441536 | bytes 12748800 | tf_op jit(solution)/shard_map/dot_general | solution.py:391
  179.4 39.7 %shard_map.116 = f32[32,4096]{1,0:T(8,128)S(1)} custom-call(bf16[256,8192]{1,0:T(8,128)(2,1)S(1)} %fusion.2.slope, bf16[4096,8192]{1,0:T(8,128)(2,1)} %head.1, f32[32,4096]{1,0:T(8,128)S(1)} %get-tuple-element.6.hidden_ref, f32[1,4096]{1,0:T(1,128)S(1)} %bitcast.28), custom_call_target="tpu_custom_call" | custom-call | tf_op jit(solution)/shard_map/pallas_call | solution.py:256
  219.1 0.8 copy.13
  (1 shorter events, 0.0 us)
Async XLA Ops:
  2.2 1.0 copy-start.1
  3.2 0.7 copy-start.4
  35.5 12.8 %copy-start.2 = (bf16[32,4096]{1,0:T(8,128)(2,1)S(1)}, bf16[32,4096]{1,0:T(8,128)(2,1)}, u32[]{:S(2)}) copy-start(bf16[32,4096]{1,0:T(8,128)(2,1)} %rows_ref.3) | copy-start | bytes 786436
  35.5 12.8 %copy-start.3 = (f32[4096]{0:T(1024)S(1)}, f32[4096]{0:T(1024)}, u32[]{:S(2)}) copy-start(f32[4096]{0:T(1024)} %param.14) | copy-start | bytes 49156
  48.3 2.2 copy-start
  102.7 29.7 %copy-start.5 = (s32[1,256]{1,0:T(1,128)S(1)}, s32[1,256]{1,0:T(1,128)}, u32[]{:S(2)}) copy-start(s32[1,256]{1,0:T(1,128)} %param.16) | copy-start | bytes 3076
